TPU v7x, 512 devices: a whole 4x4x16 slice. The times are simulated.
512 devices in a mesh: gx: 16 (over x, z_lo), gy: 32 (over y, z_hi, core).
Axes of the slice: x: 4, y: 4, z: 16 (z_hi: 4, z_lo: 4; z = z_hi * 4 + z_lo), core: 2. Of those that a mesh axis runs over, the one named last changes fastest.
Arguments:
- populations: float32 [19, 2, 128, 4096], P(None, None, 'gx', 'gy'), may hold values from 0.3 to 2.3, as said below
- labels: int32 [2, 128, 4096], P(None, 'gx', 'gy'), may hold values 0 or 1
- solid: int32 [2, 128, 4096], P(None, 'gx', 'gy'), may hold values 0 or 1
- rates: float32 [15], replicated, may hold values from 0.7 to 1.8
Outputs:
- final_state: float32 [2, 19, 2, 128, 4096], P(None, None, None, 'gx', 'gy')
Inputs may be any that keep to these rules, and one draw needn't show every extreme that they name: `populations`: each value is a population divided by its lattice weight, near equilibrium with a velocity of at most 0.05 a component and a density between 0.7 and 1.3, with a relative roughness of up to 0.3 a population.
All inputs are finite; a program needn't handle non-finite values. No bound on the sum of `labels` or of `solid` on one device may be relied on, other than what follows from the above.
Results may differ from a plain program's by a relative error of at most 0.0001.
Values sent between devices are 32-bit elements; how exact they have to be, the bound alone decides.
A program may use at most 64 MiB of HBM per device.

v0:
```python
import functools

import jax
import jax.numpy as jnp
import numpy as np
from jax import lax
from jax.experimental import pallas as pl
from jax.experimental.pallas import tpu as pltpu
from jax.sharding import PartitionSpec as P

ITERS = 6
HALO = 2 * ITERS
MESH = pl.DeviceIdType.MESH

velocity_table = np.array(
    [
        [0, 0, 0],
        [1, 0, 0],
        [-1, 0, 0],
        [0, 1, 0],
        [0, -1, 0],
        [0, 0, 1],
        [0, 0, -1],
        [1, 1, 0],
        [-1, -1, 0],
        [1, -1, 0],
        [-1, 1, 0],
        [1, 0, 1],
        [-1, 0, -1],
        [1, 0, -1],
        [-1, 0, 1],
        [0, 1, 1],
        [0, -1, -1],
        [0, 1, -1],
        [0, -1, 1],
    ]
)
half_tension = 0.05
recolor_beta = 0.7
gradient_floor = 0.1
ROWS = 8
LANES = 128
EXTENT = ROWS + 2 * HALO
CHUNK = 16
PER_PLANE = LANES // CHUNK
PLANES = 42
PACKED = -(-PLANES // PER_PLANE)


def opposite_of(member):
    return int(np.argmax(np.all(velocity_table == -velocity_table[member], axis=1)))


OPPOSITE = [opposite_of(member) for member in range(19)]


def placement(dx):
    first = HALO - ROWS * dx
    low, high = max(first, 0), min(first + ROWS, EXTENT)
    return low - first, low, high - low


def gather_kernel(pop_hbm, flag_hbm, ext_ref, flags_ref, strip_ref, pop, flag, right, left, send, recv, local):
    gx, gy = lax.axis_index("gx"), lax.axis_index("gy")
    nx, ny = lax.axis_size("gx"), lax.axis_size("gy")
    offsets = [(dx, dy) for dy in (1, -1) for dx in (1, -1, 0, 2, -2)] + [(1, 0), (-1, 0), (2, 0), (-2, 0)]
    device = {
        (dx, dy): (lax.rem(gx + (dx + nx), nx), lax.rem(gy + (dy + ny), ny)) for dx, dy in offsets
    }
    barrier = pltpu.get_barrier_semaphore()
    for offset in offsets:
        pl.semaphore_signal(barrier, inc=1, device_id=device[offset], device_id_type=MESH)
    loads = [
        pltpu.make_async_copy(pop_hbm, pop, local.at[0]),
        pltpu.make_async_copy(flag_hbm, flag, local.at[1]),
    ]
    for copy in loads:
        copy.start()
    for copy in loads:
        copy.wait()
    keep = [
        pltpu.make_async_copy(pop, ext_ref.at[:, :, HALO : HALO + ROWS, :], local.at[2]),
        pltpu.make_async_copy(flag, flags_ref.at[:, :, HALO : HALO + ROWS, :], local.at[3]),
    ]
    for copy in keep:
        copy.start()

    chunk = lax.broadcasted_iota(jnp.int32, (ROWS, LANES), 1) // CHUNK
    for first in range(0, PLANES, PER_PLANE):
        to_left = to_right = None
        for slot in range(min(PER_PLANE, PLANES - first)):
            plane = first + slot
            value = pop[plane // 2, plane % 2] if plane < 38 else flag[(plane - 38) // 2, plane % 2]
            moved = value if slot == 0 else pltpu.roll(value, CHUNK * slot, 1)
            to_left = moved if slot == 0 else jnp.where(chunk == slot, moved, to_left)
            before = (slot - 1) % PER_PLANE
            to_right = moved if slot == 0 else jnp.where(chunk == before, moved, to_right)
        left[first // PER_PLANE] = to_left
        right[first // PER_PLANE] = to_right

    pl.semaphore_wait(barrier, len(offsets))
    copies = []

    def push(source, target, device_id):
        number = len(copies)
        copy = pltpu.make_async_remote_copy(
            src_ref=source,
            dst_ref=target,
            send_sem=send.at[number],
            recv_sem=recv.at[number],
            device_id=device_id,
            device_id_type=MESH,
        )
        copy.start()
        copies.append(copy)

    for dx, dy in offsets:
        begin, low, count = placement(dx)
        if dy != 0:
            source = right if dy > 0 else left
            push(
                source.at[:, begin : begin + count, :],
                strip_ref.at[0 if dy > 0 else 1, :, low : low + count, :],
                device[dx, dy],
            )
            continue
        push(
            flag.at[:, :, begin : begin + count, :],
            flags_ref.at[:, :, low : low + count, :],
            device[dx, dy],
        )
        if dx == 2:
            begin, low, count = begin + 1, low + 1, count - 1
        if dx == -2:
            count = count - 1
        push(
            pop.at[:, :, begin : begin + count, :],
            ext_ref.at[:, :, low : low + count, :],
            device[dx, dy],
        )
    for copy in keep:
        copy.wait()
    for copy in copies:
        copy.wait_recv()
    for copy in copies:
        copy.wait_send()


def gather(populations, flags):
    shapes = [
        jax.ShapeDtypeStruct((19, 2, EXTENT, LANES), jnp.float32),
        jax.ShapeDtypeStruct((2, 2, EXTENT, LANES), jnp.float32),
        jax.ShapeDtypeStruct((2, PACKED, EXTENT, LANES), jnp.float32),
    ]
    anywhere = pl.BlockSpec(memory_space=pl.ANY)
    return pl.pallas_call(
        gather_kernel,
        out_shape=shapes,
        in_specs=[anywhere] * 2,
        out_specs=[anywhere] * 3,
        scratch_shapes=[
            pltpu.VMEM((19, 2, ROWS, LANES), jnp.float32),
            pltpu.VMEM((2, 2, ROWS, LANES), jnp.float32),
            pltpu.VMEM((PACKED, ROWS, LANES), jnp.float32),
            pltpu.VMEM((PACKED, ROWS, LANES), jnp.float32),
            pltpu.SemaphoreType.DMA((18,)),
            pltpu.SemaphoreType.DMA((18,)),
            pltpu.SemaphoreType.DMA((4,)),
        ],
        compiler_params=pltpu.CompilerParams(collective_id=0, has_side_effects=True),
    )(populations, flags)


def lateral(pair, dy, lane):
    if dy == 0:
        return pair
    edge = lane == (LANES - 1 if dy > 0 else 0)
    return [
        pltpu.roll(jnp.where(edge, pair[1 - part], pair[part]), dy % LANES, 1) for part in range(2)
    ]


def relax(f, rate):
    plus = {q: f[q] + f[q + 1] for q in range(1, 19, 2)}
    minus = {q: f[q] - f[q + 1] for q in range(1, 19, 2)}
    both = {q: plus[q] + plus[q + 2] for q in (7, 11, 15)}
    cross = {q: plus[q] - plus[q + 2] for q in (7, 11, 15)}
    head = {q: minus[q] + minus[q + 2] for q in (7, 11, 15)}
    tail = {q: minus[q] - minus[q + 2] for q in (7, 11, 15)}
    axes = plus[1] + plus[3] + plus[5]
    diagonals = both[7] + both[11] + both[15]
    density = f[0] * (1.0 / 3.0) + axes * (1.0 / 18.0) + diagonals * (1.0 / 36.0)
    momentum = [
        minus[1] * (1.0 / 18.0) + (head[7] + head[11]) * (1.0 / 36.0),
        minus[3] * (1.0 / 18.0) + (tail[7] + head[15]) * (1.0 / 36.0),
        minus[5] * (1.0 / 18.0) + (tail[11] + tail[15]) * (1.0 / 36.0),
    ]
    inverse = 1.0 / density
    speed = [part * inverse for part in momentum]
    xx, yy, zz = (momentum[k] * speed[k] for k in range(3))
    xy, yz, xz = momentum[0] * speed[1], momentum[1] * speed[2], momentum[0] * speed[2]
    square = xx + yy + zz
    energy = f[0] * -10.0 + axes * (-11.0 / 18.0) + diagonals * (8.0 / 36.0) - (19.0 * square - 11.0 * density)
    fourth = f[0] * 4.0 + axes * (-4.0 / 18.0) + diagonals * (1.0 / 36.0) - (3.0 * density - 5.5 * square)
    first_axis = (3.0 * plus[1] - axes) * (1.0 / 18.0)
    first_diag = (diagonals - 3.0 * both[15]) * (1.0 / 36.0)
    first_flow = 3.0 * xx - square
    second_axis = (plus[3] - plus[5]) * (1.0 / 18.0)
    second_diag = (both[7] - both[11]) * (1.0 / 36.0)
    second_flow = yy - zz
    energy = energy * (rate[0] * (1.0 / 2394.0))
    fourth = fourth * (rate[1] * (1.0 / 252.0))
    first = (first_axis + first_diag - first_flow) * (rate[5] * (1.0 / 36.0))
    first_high = (first_diag - 2.0 * first_axis + 0.5 * first_flow) * (rate[6] * (1.0 / 72.0))
    second = (second_axis + second_diag - second_flow) * (rate[7] * (1.0 / 12.0))
    second_high = (second_diag - 2.0 * second_axis + 0.5 * second_flow) * (rate[8] * (1.0 / 24.0))
    on_rest = energy * -90.0 + fourth * 36.0
    on_axes = energy * -198.0 - fourth * 72.0
    on_diagonals = energy * 288.0 + fourth * 36.0
    axis_first = (first - 2.0 * first_high) * 18.0
    axis_second = (second - 2.0 * second_high) * 18.0
    diag_first = (first + first_high) * 36.0
    diag_second = (second + second_high) * 36.0
    rest_axes = on_axes - axis_first
    along = [on_axes + 2.0 * axis_first, rest_axes + axis_second, rest_axes - axis_second]
    near = on_diagonals + diag_first
    around = {7: near + diag_second, 11: near - diag_second, 15: on_diagonals - 2.0 * diag_first}
    shear = {
        7: (cross[7] * (1.0 / 36.0) - xy) * (rate[9] * 9.0),
        15: (cross[15] * (1.0 / 36.0) - yz) * (rate[10] * 9.0),
        11: (cross[11] * (1.0 / 36.0) - xz) * (rate[11] * 9.0),
    }
    flux = []
    for k, diag in enumerate((head[7] + head[11], tail[7] + head[15], tail[11] + tail[15])):
        moment = minus[2 * k + 1] * (-4.0 / 18.0) + diag * (1.0 / 36.0) + momentum[k] * (2.0 / 3.0)
        flux.append(moment * (rate[2 + k] * 0.9))
    twist = [
        (head[7] - head[11]) * (rate[12] * (4.5 / 36.0)),
        (head[15] - tail[7]) * (rate[13] * (4.5 / 36.0)),
        (tail[11] - tail[15]) * (rate[14] * (4.5 / 36.0)),
    ]
    left = [None] * 19
    left[0] = f[0] - on_rest
    for k in range(3):
        double = 2.0 * flux[k]
        left[2 * k + 1] = f[2 * k + 1] - (along[k] - double)
        left[2 * k + 2] = f[2 * k + 2] - (along[k] + double)
    odd = {
        7: (flux[0] + twist[0], flux[1] - twist[1]),
        11: (flux[0] - twist[0], flux[2] + twist[2]),
        15: (flux[1] + twist[1], flux[2] - twist[2]),
    }
    for q in (7, 11, 15):
        same, other = around[q] + shear[q], around[q] - shear[q]
        total, gap = odd[q][0] + odd[q][1], odd[q][0] - odd[q][1]
        left[q] = f[q] - (same + total)
        left[q + 1] = f[q + 1] - (same - total)
        left[q + 2] = f[q + 2] - (other + gap)
        left[q + 3] = f[q + 3] - (other - gap)
    return density, inverse, left


def weighted_sum(f):
    axes = functools.reduce(lambda a, b: a + b, f[1:7])
    diagonals = functools.reduce(lambda a, b: a + b, f[7:19])
    return f[0] * (1.0 / 3.0) + axes * (1.0 / 18.0) + diagonals * (1.0 / 36.0)


def windows(low, high):
    count = -(-(high - low) // ROWS)
    return count, high - ROWS


def steps_kernel(rate_ref, ext, flags, strips, out, left_ref, frac_ref, mix_ref, total_ref, red_ref, label_ref, rock_ref):
    rate = [rate_ref[k] for k in range(15)]
    lane = lax.broadcasted_iota(jnp.int32, (ROWS, LANES), 1)
    right_half = lane < LANES // 2

    def rows_of(index, low, high):
        return jnp.minimum(low + ROWS * index, high - ROWS)

    def keep(d, part, rows, density, share, remains):
        frac_ref[d, part, rows, :] = share
        mix_ref[d, part, rows, :] = recolor_beta * density * share * (1.0 - share)
        for q in range(19):
            left_ref[q, d, part, rows, :] = remains[q]

    def start(index, carry):
        w, d = index // 2, lax.rem(index, 2)
        rows = pl.ds(pl.multiple_of(w * ROWS, ROWS), ROWS)

        def strip(plane):
            first, second = [], []
            for depth in range(2):
                number = 2 * plane + depth
                which, slot = number // PER_PLANE, number % PER_PLANE
                moved = [strips[side, which, rows, :] for side in range(2)]
                if slot:
                    moved = [pltpu.roll(value, LANES - CHUNK * slot, 1) for value in moved]
                first.append(jnp.where(right_half, moved[1], moved[0]))
            return jnp.where(d == 0, first[0], first[1])

        label = [flags[0, d, rows, :], strip(19)]
        rock = [flags[1, d, rows, :], strip(20)]
        for dy in (-1, 0, 1):
            moved = lateral(rock, dy, lane)
            for part in range(2):
                rock_ref[dy + 1, d, part, rows, :] = moved[part]
        for part in range(2):
            label_ref[d, part, rows, :] = label[part]
        f = [[ext[q, d, rows, :] for q in range(19)], [strip(q) for q in range(19)]]
        for part in range(2):
            density, _, remains = relax(f[part], rate)
            keep(d, part, rows, density, label[part], remains)
        return carry

    lax.fori_loop(0, 2 * (EXTENT // ROWS), start, 0)

    def collide(low, high, index, carry):
        w, d = index // 2, lax.rem(index, 2)
        row = rows_of(w, low, high)
        here = pl.ds(row, ROWS)
        mine, theirs = {}, {}
        for dx in (-1, 0, 1):
            rows = pl.ds(row + dx, ROWS)
            mine[dx] = [frac_ref[d, part, rows, :] for part in range(2)]
            theirs[dx] = [frac_ref[1 - d, part, rows, :] for part in range(2)]
        planes = {dx: [(mine[dx][k] + theirs[dx][k]) * (1.0 / 3.0) for k in range(2)] for dx in (-1, 0, 1)}
        slope = [(mine[1][k] - mine[-1][k]) * (1.0 / 6.0) for k in range(2)]
        ahead, behind = lateral(slope, -1, lane), lateral(slope, 1, lane)
        level = [planes[0][k] + (mine[1][k] + mine[-1][k]) * (1.0 / 6.0) for k in range(2)]
        after, before = lateral(level, -1, lane), lateral(level, 1, lane)
        for part in range(2):
            gx = planes[1][part] - planes[-1][part] + ahead[part] + behind[part]
            gy = after[part] - before[part]
            both, gap = gx + gy, gx - gy
            magnitude = jnp.sqrt(gx * gx + gy * gy)
            inverse = 1.0 / jnp.maximum(magnitude, gradient_floor)
            pull = half_tension * magnitude
            scale = half_tension * inverse
            added = {
                (0, 0): -pull,
                (1, 0): gx * gx * scale - pull,
                (0, 1): gy * gy * scale - pull,
                (1, 1): both * both * scale - pull,
                (1, -1): gap * gap * scale - pull,
            }
            share = mine[0][part]
            mixing = mix_ref[d, part, here, :] * inverse
            diagonal = mixing * float(1.0 / np.sqrt(2.0))
            turned = {
                (1, 0, 0): mixing * gx,
                (0, 1, 0): mixing * gy,
                (1, 1, 0): diagonal * both,
                (1, -1, 0): diagonal * gap,
                (1, 0, 1): diagonal * gx,
                (0, 1, 1): diagonal * gy,
            }
            for q in range(19):
                a, b, c = (int(v) for v in velocity_table[q])
                remains = left_ref[q, d, part, here, :]
                sign = 1 if (a, b) > (0, 0) else -1
                key = (a * sign, b * sign) if (a, b) != (0, 0) else (0, 0)
                value = remains + pull if q == 0 else remains + added[key]
                total_ref[q, d, part, here, :] = value
                red = share * value
                if key != (0, 0):
                    turn = turned[key[0], key[1], abs(c)]
                    red = red + turn if sign > 0 else red - turn
                red_ref[q, d, part, here, :] = red
        return carry

    def stream(row, d, parts):
        here = pl.ds(row, ROWS)
        totals, reds = [[], []], [[], []]
        for q in range(19):
            a, b, c = (int(v) for v in velocity_table[q])
            rows = pl.ds(row - a, ROWS)
            source = d if c == 0 else 1 - d
            for ref, found in ((total_ref, totals), (red_ref, reds)):
                if b == 0:
                    moved = [ref[q, source, part, rows, :] for part in range(parts)]
                else:
                    pair = [ref[q, source, part, rows, :] for part in range(2)]
                    edge = lane == (LANES - 1 if b > 0 else 0)
                    moved = [
                        pltpu.roll(jnp.where(edge, pair[1 - part], pair[part]), b % LANES, 1)
                        for part in range(parts)
                    ]
                for part in range(parts):
                    value = moved[part]
                    if q:
                        wall = rock_ref[b + 1, source, part, rows, :] > 0.5
                        value = jnp.where(wall, ref[OPPOSITE[q], d, part, here, :], value)
                    found[part].append(value)
        return totals, reds

    def advance(low, high, index, carry):
        w, d = index // 2, lax.rem(index, 2)
        row = rows_of(w, low, high)
        here = pl.ds(row, ROWS)
        totals, reds = stream(row, d, 2)
        for part in range(2):
            density, inverse, remains = relax(totals[part], rate)
            rock = rock_ref[1, d, part, here, :] > 0.5
            label = label_ref[d, part, here, :]
            share = jnp.where(rock, label, weighted_sum(reds[part]) * inverse)
            keep(d, part, here, density, share, remains)
        return carry

    for step in range(ITERS):
        low, high = 2 * step + 1, EXTENT - 2 * step - 1
        lax.fori_loop(0, 2 * windows(low, high)[0], functools.partial(collide, low, high), 0)
        low, high = low + 1, high - 1
        if step < ITERS - 1:
            lax.fori_loop(0, 2 * windows(low, high)[0], functools.partial(advance, low, high), 0)

    def finish(d, carry):
        totals, reds = stream(HALO, d, 1)
        here = pl.ds(HALO, ROWS)
        rock = rock_ref[1, d, 0, here, :] > 0.5
        label = label_ref[d, 0, here, :]
        for q in range(19):
            first = ext[q, d, here, :]
            out[0, q, d] = jnp.where(rock, first, totals[0][q])
            out[1, q, d] = jnp.where(rock, label * first, reds[0][q])
        return carry

    lax.fori_loop(0, 2, finish, 0)


def steps(rates, ext, flags, strips):
    whole = pl.BlockSpec(memory_space=pltpu.VMEM)
    field = (2, 2, EXTENT, LANES)
    return pl.pallas_call(
        steps_kernel,
        out_shape=jax.ShapeDtypeStruct((2, 19, 2, ROWS, LANES), jnp.float32),
        in_specs=[pl.BlockSpec(memory_space=pltpu.SMEM)] + [whole] * 3,
        out_specs=whole,
        scratch_shapes=[
            pltpu.VMEM((19,) + field, jnp.float32),
            pltpu.VMEM(field, jnp.float32),
            pltpu.VMEM(field, jnp.float32),
            pltpu.VMEM((19,) + field, jnp.float32),
            pltpu.VMEM((19,) + field, jnp.float32),
            pltpu.VMEM(field, jnp.float32),
            pltpu.VMEM((3,) + field, jnp.float32),
        ],
        compiler_params=pltpu.CompilerParams(vmem_limit_bytes=32 * 2**20),
    )(rates, ext, flags, strips)


def body(populations, labels, solid, rates):
    flags = jnp.stack([labels, (solid > 0).astype(labels.dtype)]).astype(jnp.float32)
    ext, flags, strips = gather(populations, flags)
    return steps(rates, ext, flags, strips)


def solution(mesh):
    return jax.shard_map(
        body,
        mesh=mesh,
        in_specs=(P(None, None, "gx", "gy"), P(None, "gx", "gy"), P(None, "gx", "gy"), P()),
        out_specs=P(None, None, None, "gx", "gy"),
        check_vma=False,
    )
```

profile of v0, /device:TPU:24, one launch (start us, length us, event | category | flops | bytes accessed | tf_op | source)
XLA Modules:
  0.0 52.9 jit_solution(11465401045074640637)
XLA Ops:
  0.0 0.0 copy-start.4
  0.0 0.7 %convert_bitcast_fusion = s32[1,2,8,128]{3,2,1,0:T(8,128)S(1)} fusion(s32[2,8,128]{2,1,0:T(8,128)} %param.6), kind=kLoop, calls=%fused_computation.1 | loop fusion | flops 4096 | bytes 16384 | tf_op jit(solution)/shard_map/stack | solution.py:454
  0.7 0.0 copy-done.4
  0.7 0.6 %add_convert_fusion.flag_hbm = f32[2,2,8,128]{3,2,1,0:T(8,128)} fusion(s32[1,2,8,128]{3,2,1,0:T(8,128)S(1)} %convert_bitcast_fusion, s32[1,2,8,128]{3,2,1,0:T(8,128)S(1)} %bitcast.3), kind=kLoop, calls=%fused_computation | loop fusion | flops 8192 | bytes 32768 | tf_op jit(solution)/shard_map/convert_element_type | solution.py:454
  1.3 34.9 %shard_map.46 = (f32[19,2,32,128]{3,2,1,0:T(8,128)}, f32[2,2,32,128]{3,2,1,0:T(8,128)}, f32[2,6,32,128]{3,2,1,0:T(8,128)}) custom-call(f32[19,2,8,128]{3,2,1,0:T(8,128)} %pop_hbm.1, f32[2,2,8,128]{3,2,1,0:T(8,128)} %add_convert_fusion.flag_hbm), custom_call_target="tpu_custom_call" | custom-call | tf_op jit(solution)/shard_map/pallas_call | solution.py:156
  36.2 0.0 copy-start.3
  36.3 0.6 %copy-done.3 = f32[15]{0:T(128)S(1)} copy-done((f32[15]{0:T(128)S(1)}, f32[15]{0:T(128)}, u32[]{:S(2)}) %copy-start.3) | copy-done | bytes 84
  36.9 0.0 copy-start
  36.9 1.1 %copy-done = f32[19,2,32,128]{3,2,1,0:T(8,128)S(1)} copy-done((f32[19,2,32,128]{3,2,1,0:T(8,128)S(1)}, f32[19,2,32,128]{3,2,1,0:T(8,128)}, u32[]{:S(2)}) %copy-start) | copy-done | bytes 622616
  38.0 0.0 copy-start.1
  38.0 0.9 %copy-done.1 = f32[2,6,32,128]{3,2,1,0:T(8,128)S(1)} copy-done((f32[2,6,32,128]{3,2,1,0:T(8,128)S(1)}, f32[2,6,32,128]{3,2,1,0:T(8,128)}, u32[]{:S(2)}) %copy-start.1) | copy-done | bytes 196632
  38.9 0.0 copy-start.2
  38.9 0.8 %copy-done.2 = f32[2,2,32,128]{3,2,1,0:T(8,128)S(1)} copy-done((f32[2,2,32,128]{3,2,1,0:T(8,128)S(1)}, f32[2,2,32,128]{3,2,1,0:T(8,128)}, u32[]{:S(2)}) %copy-start.2) | copy-done | bytes 65560
  39.7 13.2 %shard_map.47 = f32[2,19,2,8,128]{4,3,2,1,0:T(8,128)} custom-call(f32[15]{0:T(128)S(1)} %copy-done.3, f32[19,2,32,128]{3,2,1,0:T(8,128)S(1)} %copy-done, f32[2,2,32,128]{3,2,1,0:T(8,128)S(1)} %copy-done.2, f32[2,6,32,128]{3,2,1,0:T(8,128)S(1)} %copy-done.1), custom_call_target="tpu_custom_call" | custom-call | tf_op jit(solution)/shard_map/pallas_call | solution.py:435
Async XLA Ops:
  0.0 0.7 %copy-start.4 = (s32[2,8,128]{2,1,0:T(8,128)S(1)}, s32[2,8,128]{2,1,0:T(8,128)}, u32[]{:S(2)}) copy-start(s32[2,8,128]{2,1,0:T(8,128)} %param.5) | copy-start | bytes 24580
  36.2 0.7 %copy-start.3 = (f32[15]{0:T(128)S(1)}, f32[15]{0:T(128)}, u32[]{:S(2)}) copy-start(f32[15]{0:T(128)} %rate_ref.1) | copy-start | bytes 184
  36.9 1.1 %copy-start = (f32[19,2,32,128]{3,2,1,0:T(8,128)S(1)}, f32[19,2,32,128]{3,2,1,0:T(8,128)}, u32[]{:S(2)}) copy-start(f32[19,2,32,128]{3,2,1,0:T(8,128)} %get-tuple-element.8.ext) | copy-start | bytes 1867780
  38.0 0.9 %copy-start.1 = (f32[2,6,32,128]{3,2,1,0:T(8,128)S(1)}, f32[2,6,32,128]{3,2,1,0:T(8,128)}, u32[]{:S(2)}) copy-start(f32[2,6,32,128]{3,2,1,0:T(8,128)} %get-tuple-element.10.strips) | copy-start | bytes 589828
  38.9 0.8 %copy-start.2 = (f32[2,2,32,128]{3,2,1,0:T(8,128)S(1)}, f32[2,2,32,128]{3,2,1,0:T(8,128)}, u32[]{:S(2)}) copy-start(f32[2,2,32,128]{3,2,1,0:T(8,128)} %get-tuple-element.9.flags) | copy-start | bytes 196612
where the time goes:
time: 53.2 us; the launch traced here: 52.9 us
  Pallas kernels  48.1 us (90%)
  local copies, waits for them, and re-layouts  3.49 us (7%)
  other arithmetic  1.32 us (2%)
    pallas_call x1, Pallas kernels, gather(): pl.pallas_call(gather_kernel, out_shape=shapes, in_specs=[anywhere] * 2,...  34.9 us
    pallas_call x1, Pallas kernels, steps(): pl.pallas_call(steps_kernel, out_shape=jax.ShapeDtypeStruct((2, 19, 2, RO...  13.2 us
    unnamed x10, local copies, waits for them, and re-layouts  3.49 us

commit v1 on v0

v1 whole, which is shorter than its diff:
```python
import functools

import jax
import jax.numpy as jnp
import numpy as np
from jax import lax
from jax.experimental import pallas as pl
from jax.experimental.pallas import tpu as pltpu
from jax.sharding import PartitionSpec as P

ITERS = 6
ROUNDS = 2
STEPS = ITERS // ROUNDS
HALO = 2 * STEPS
MESH = pl.DeviceIdType.MESH

velocity_table = np.array(
    [
        [0, 0, 0],
        [1, 0, 0],
        [-1, 0, 0],
        [0, 1, 0],
        [0, -1, 0],
        [0, 0, 1],
        [0, 0, -1],
        [1, 1, 0],
        [-1, -1, 0],
        [1, -1, 0],
        [-1, 1, 0],
        [1, 0, 1],
        [-1, 0, -1],
        [1, 0, -1],
        [-1, 0, 1],
        [0, 1, 1],
        [0, -1, -1],
        [0, 1, -1],
        [0, -1, 1],
    ]
)
half_tension = 0.05
recolor_beta = 0.7
gradient_floor = 0.1
ROWS = 8
LANES = 128
EXTENT = ROWS + 2 * HALO
CHUNK = 8
PER_STRIP = LANES // CHUNK
FIELDS = 21
PACKED = -(-2 * FIELDS // PER_STRIP)
OWN = slice(HALO, HALO + ROWS)


def opposite_of(member):
    return int(np.argmax(np.all(velocity_table == -velocity_table[member], axis=1)))


OPPOSITE = [opposite_of(member) for member in range(19)]


def placement(dx):
    first = HALO - ROWS * dx
    low, high = max(first, 0), min(first + ROWS, EXTENT)
    return low - first, low, high - low


def lateral(pair, dy, lane):
    if dy == 0:
        return pair
    edge = lane == (LANES - 1 if dy > 0 else 0)
    return [
        pltpu.roll(jnp.where(edge, pair[1 - part], pair[part]), dy % LANES, 1) for part in range(2)
    ]


def relax(f, rate):
    plus = {q: f[q] + f[q + 1] for q in range(1, 19, 2)}
    minus = {q: f[q] - f[q + 1] for q in range(1, 19, 2)}
    both = {q: plus[q] + plus[q + 2] for q in (7, 11, 15)}
    cross = {q: plus[q] - plus[q + 2] for q in (7, 11, 15)}
    head = {q: minus[q] + minus[q + 2] for q in (7, 11, 15)}
    tail = {q: minus[q] - minus[q + 2] for q in (7, 11, 15)}
    axes = plus[1] + plus[3] + plus[5]
    diagonals = both[7] + both[11] + both[15]
    density = f[0] * (1.0 / 3.0) + axes * (1.0 / 18.0) + diagonals * (1.0 / 36.0)
    momentum = [
        minus[1] * (1.0 / 18.0) + (head[7] + head[11]) * (1.0 / 36.0),
        minus[3] * (1.0 / 18.0) + (tail[7] + head[15]) * (1.0 / 36.0),
        minus[5] * (1.0 / 18.0) + (tail[11] + tail[15]) * (1.0 / 36.0),
    ]
    inverse = 1.0 / density
    speed = [part * inverse for part in momentum]
    xx, yy, zz = (momentum[k] * speed[k] for k in range(3))
    xy, yz, xz = momentum[0] * speed[1], momentum[1] * speed[2], momentum[0] * speed[2]
    square = xx + yy + zz
    energy = f[0] * -10.0 + axes * (-11.0 / 18.0) + diagonals * (8.0 / 36.0) - (19.0 * square - 11.0 * density)
    fourth = f[0] * 4.0 + axes * (-4.0 / 18.0) + diagonals * (1.0 / 36.0) - (3.0 * density - 5.5 * square)
    first_axis = (3.0 * plus[1] - axes) * (1.0 / 18.0)
    first_diag = (diagonals - 3.0 * both[15]) * (1.0 / 36.0)
    first_flow = 3.0 * xx - square
    second_axis = (plus[3] - plus[5]) * (1.0 / 18.0)
    second_diag = (both[7] - both[11]) * (1.0 / 36.0)
    second_flow = yy - zz
    energy = energy * (rate[0] * (1.0 / 2394.0))
    fourth = fourth * (rate[1] * (1.0 / 252.0))
    first = (first_axis + first_diag - first_flow) * (rate[5] * (1.0 / 36.0))
    first_high = (first_diag - 2.0 * first_axis + 0.5 * first_flow) * (rate[6] * (1.0 / 72.0))
    second = (second_axis + second_diag - second_flow) * (rate[7] * (1.0 / 12.0))
    second_high = (second_diag - 2.0 * second_axis + 0.5 * second_flow) * (rate[8] * (1.0 / 24.0))
    on_rest = energy * -90.0 + fourth * 36.0
    on_axes = energy * -198.0 - fourth * 72.0
    on_diagonals = energy * 288.0 + fourth * 36.0
    axis_first = (first - 2.0 * first_high) * 18.0
    axis_second = (second - 2.0 * second_high) * 18.0
    diag_first = (first + first_high) * 36.0
    diag_second = (second + second_high) * 36.0
    rest_axes = on_axes - axis_first
    along = [on_axes + 2.0 * axis_first, rest_axes + axis_second, rest_axes - axis_second]
    near = on_diagonals + diag_first
    around = {7: near + diag_second, 11: near - diag_second, 15: on_diagonals - 2.0 * diag_first}
    shear = {
        7: (cross[7] * (1.0 / 36.0) - xy) * (rate[9] * 9.0),
        15: (cross[15] * (1.0 / 36.0) - yz) * (rate[10] * 9.0),
        11: (cross[11] * (1.0 / 36.0) - xz) * (rate[11] * 9.0),
    }
    flux = []
    for k, diag in enumerate((head[7] + head[11], tail[7] + head[15], tail[11] + tail[15])):
        moment = minus[2 * k + 1] * (-4.0 / 18.0) + diag * (1.0 / 36.0) + momentum[k] * (2.0 / 3.0)
        flux.append(moment * (rate[2 + k] * 0.9))
    twist = [
        (head[7] - head[11]) * (rate[12] * (4.5 / 36.0)),
        (head[15] - tail[7]) * (rate[13] * (4.5 / 36.0)),
        (tail[11] - tail[15]) * (rate[14] * (4.5 / 36.0)),
    ]
    left = [None] * 19
    left[0] = f[0] - on_rest
    for k in range(3):
        double = 2.0 * flux[k]
        left[2 * k + 1] = f[2 * k + 1] - (along[k] - double)
        left[2 * k + 2] = f[2 * k + 2] - (along[k] + double)
    odd = {
        7: (flux[0] + twist[0], flux[1] - twist[1]),
        11: (flux[0] - twist[0], flux[2] + twist[2]),
        15: (flux[1] + twist[1], flux[2] - twist[2]),
    }
    for q in (7, 11, 15):
        same, other = around[q] + shear[q], around[q] - shear[q]
        total, gap = odd[q][0] + odd[q][1], odd[q][0] - odd[q][1]
        left[q] = f[q] - (same + total)
        left[q + 1] = f[q + 1] - (same - total)
        left[q + 2] = f[q + 2] - (other + gap)
        left[q + 3] = f[q + 3] - (other - gap)
    return density, inverse, left


def weighted_sum(f):
    axes = functools.reduce(lambda a, b: a + b, f[1:7])
    diagonals = functools.reduce(lambda a, b: a + b, f[7:19])
    return f[0] * (1.0 / 3.0) + axes * (1.0 / 18.0) + diagonals * (1.0 / 36.0)


def over_windows(low, high, work):
    count = -(-(high - low) // ROWS)
    if count == 1:
        work(low)
        return

    def one(index, carry):
        work(jnp.minimum(low + ROWS * index, high - ROWS))
        return carry

    lax.fori_loop(0, count, one, 0)


def kernel(
    rate_ref, pop_hbm, label_hbm, solid_hbm, out, *scratch
):
    states, strips = scratch[:ROUNDS], scratch[ROUNDS : 2 * ROUNDS]
    packs, codes, left_ref, frac_ref, mix_ref, total_ref, red_ref, label_ref, rock_ref, send, recv, local = scratch[2 * ROUNDS :]
    gx, gy = lax.axis_index("gx"), lax.axis_index("gy")
    nx, ny = lax.axis_size("gx"), lax.axis_size("gy")
    offsets = [(dx, dy) for dy in (1, -1) for dx in (1, -1, 0)] + [(1, 0), (-1, 0)]
    device = {
        (dx, dy): (lax.rem(gx + (dx + nx), nx), lax.rem(gy + (dy + ny), ny)) for dx, dy in offsets
    }
    barrier = pltpu.get_barrier_semaphore()
    for offset in offsets:
        pl.semaphore_signal(barrier, inc=1, device_id=device[offset], device_id_type=MESH)
    loads = [
        pltpu.make_async_copy(label_hbm, codes.at[0], local.at[1]),
        pltpu.make_async_copy(solid_hbm, codes.at[1], local.at[2]),
        pltpu.make_async_copy(pop_hbm, states[0].at[0:19, :, OWN, :], local.at[0]),
    ]
    for copy in loads:
        copy.start()
    for copy in loads:
        copy.wait()
    for d in range(2):
        states[0][19, d, OWN, :] = codes[0, d].astype(jnp.float32)
        states[0][20, d, OWN, :] = jnp.where(codes[1, d] > 0, 1.0, 0.0)

    rate = [rate_ref[k] for k in range(15)]
    lane = lax.broadcasted_iota(jnp.int32, (ROWS, LANES), 1)
    chunk = lane // CHUNK
    right_half = lane < LANES // 2

    def pack(number, fields):
        for first in range(0, 2 * fields, PER_STRIP):
            to_left = to_right = None
            for slot in range(min(PER_STRIP, 2 * fields - first)):
                plane = first + slot
                value = states[number][plane // 2, plane % 2, OWN, :]
                moved = value if slot == 0 else pltpu.roll(value, CHUNK * slot, 1)
                to_left = moved if slot == 0 else jnp.where(chunk == slot, moved, to_left)
                before = (slot - 1) % PER_STRIP
                to_right = moved if slot == 0 else jnp.where(chunk == before, moved, to_right)
            packs[number, 0, first // PER_STRIP] = to_right
            packs[number, 1, first // PER_STRIP] = to_left

    def exchange(number, fields):
        copies = []
        for dx, dy in offsets:
            begin, low, count = placement(dx)
            if dy != 0:
                side, used = (0 if dy > 0 else 1), -(-2 * fields // PER_STRIP)
                source = packs.at[number, side, 0:used, begin : begin + count, :]
                target = strips[number].at[side, 0:used, low : low + count, :]
            else:
                source = states[number].at[0:fields, :, HALO + begin : HALO + begin + count, :]
                target = states[number].at[0:fields, :, low : low + count, :]
            place = len(copies)
            copy = pltpu.make_async_remote_copy(
                src_ref=source,
                dst_ref=target,
                send_sem=send.at[number, place],
                recv_sem=recv.at[number, place],
                device_id=device[dx, dy],
                device_id_type=MESH,
            )
            copy.start()
            copies.append(copy)
        for copy in copies:
            copy.wait_recv()
        return copies

    def strip(number, field, d, rows):
        plane = 2 * field + d
        which, slot = plane // PER_STRIP, plane % PER_STRIP
        moved = [strips[number][side, which, rows, :] for side in range(2)]
        if slot:
            moved = [pltpu.roll(value, LANES - CHUNK * slot, 1) for value in moved]
        return jnp.where(right_half, moved[1], moved[0])

    def keep(d, part, rows, density, share, remains):
        frac_ref[d, part, rows, :] = share
        mix_ref[d, part, rows, :] = recolor_beta * density * share * (1.0 - share)
        for q in range(19):
            left_ref[q, d, part, rows, :] = remains[q]

    def start(number, row):
        rows = pl.ds(row, ROWS)
        for d in range(2):

            def both_of(field):
                return [states[number][field, d, rows, :], strip(number, field, d, rows)]

            share = both_of(19)
            if number == 0:
                rock = both_of(20)
                for dy in (-1, 0, 1):
                    moved = lateral(rock, dy, lane)
                    for part in range(2):
                        rock_ref[dy + 1, d, part, rows, :] = moved[part]
                for part in range(2):
                    label_ref[d, part, rows, :] = share[part]
            f = [both_of(q) for q in range(19)]
            for part in range(2):
                density, _, remains = relax([pair[part] for pair in f], rate)
                keep(d, part, rows, density, share[part], remains)

    def collide(row):
        here = pl.ds(row, ROWS)
        shares = {
            (d, dx): [frac_ref[d, part, pl.ds(row + dx, ROWS), :] for part in range(2)]
            for d in range(2)
            for dx in (-1, 0, 1)
        }
        planes = {
            dx: [(shares[0, dx][k] + shares[1, dx][k]) * (1.0 / 3.0) for k in range(2)] for dx in (-1, 0, 1)
        }
        for d in range(2):
            above, below = shares[d, 1], shares[d, -1]
            slope = [(above[k] - below[k]) * (1.0 / 6.0) for k in range(2)]
            ahead, behind = lateral(slope, -1, lane), lateral(slope, 1, lane)
            level = [planes[0][k] + (above[k] + below[k]) * (1.0 / 6.0) for k in range(2)]
            after, before = lateral(level, -1, lane), lateral(level, 1, lane)
            for part in range(2):
                gx = planes[1][part] - planes[-1][part] + ahead[part] + behind[part]
                gy = after[part] - before[part]
                recolor(d, part, here, shares[d, 0][part], gx, gy)

    def recolor(d, part, here, share, gx, gy):
        both, gap = gx + gy, gx - gy
        magnitude = jnp.sqrt(gx * gx + gy * gy)
        inverse = 1.0 / jnp.maximum(magnitude, gradient_floor)
        pull = half_tension * magnitude
        scale = half_tension * inverse
        added = {
            (0, 0): -pull,
            (1, 0): gx * gx * scale - pull,
            (0, 1): gy * gy * scale - pull,
            (1, 1): both * both * scale - pull,
            (1, -1): gap * gap * scale - pull,
        }
        mixing = mix_ref[d, part, here, :] * inverse
        diagonal = mixing * float(1.0 / np.sqrt(2.0))
        turned = {
            (1, 0, 0): mixing * gx,
            (0, 1, 0): mixing * gy,
            (1, 1, 0): diagonal * both,
            (1, -1, 0): diagonal * gap,
            (1, 0, 1): diagonal * gx,
            (0, 1, 1): diagonal * gy,
        }
        for q in range(19):
            a, b, c = (int(v) for v in velocity_table[q])
            remains = left_ref[q, d, part, here, :]
            sign = 1 if (a, b) > (0, 0) else -1
            key = (a * sign, b * sign) if (a, b) != (0, 0) else (0, 0)
            value = remains + pull if q == 0 else remains + added[key]
            total_ref[q, d, part, here, :] = value
            red = share * value
            if key != (0, 0):
                turn = turned[key[0], key[1], abs(c)]
                red = red + turn if sign > 0 else red - turn
            red_ref[q, d, part, here, :] = red

    def stream(row, d, parts):
        here = pl.ds(row, ROWS)
        totals, reds = [[], []], [[], []]
        for q in range(19):
            a, b, c = (int(v) for v in velocity_table[q])
            rows = pl.ds(row - a, ROWS)
            source = d if c == 0 else 1 - d
            if q:
                wall = [rock_ref[b + 1, source, part, rows, :] > 0.5 for part in range(parts)]
            for ref, found in ((total_ref, totals), (red_ref, reds)):
                if b == 0:
                    moved = [ref[q, source, part, rows, :] for part in range(parts)]
                else:
                    pair = [ref[q, source, part, rows, :] for part in range(2)]
                    edge = lane == (LANES - 1 if b > 0 else 0)
                    moved = [
                        pltpu.roll(jnp.where(edge, pair[1 - part], pair[part]), b % LANES, 1)
                        for part in range(parts)
                    ]
                for part in range(parts):
                    value = moved[part]
                    if q:
                        value = jnp.where(wall[part], ref[OPPOSITE[q], d, part, here, :], value)
                    found[part].append(value)
        return totals, reds

    def share_of(d, part, here, density_inverse, reds):
        rock = rock_ref[1, d, part, here, :] > 0.5
        return jnp.where(rock, label_ref[d, part, here, :], weighted_sum(reds) * density_inverse)

    def advance(row):
        here = pl.ds(row, ROWS)
        for d in range(2):
            totals, reds = stream(row, d, 2)
            for part in range(2):
                density, inverse, remains = relax(totals[part], rate)
                keep(d, part, here, density, share_of(d, part, here, inverse, reds[part]), remains)

    waiting = []
    for number in range(ROUNDS):
        fields = FIELDS if number == 0 else FIELDS - 1
        pack(number, fields)
        if number == 0:
            pl.semaphore_wait(barrier, len(offsets))
        waiting += exchange(number, fields)
        over_windows(0, EXTENT, functools.partial(start, number))
        for step in range(STEPS):
            low, high = 2 * step + 1, EXTENT - 2 * step - 1
            over_windows(low, high, collide)
            if step < STEPS - 1:
                over_windows(low + 1, high - 1, advance)
        for d in range(2):
            totals, reds = stream(HALO, d, 1)
            totals, reds = totals[0], reds[0]
            if number < ROUNDS - 1:
                inverse = 1.0 / weighted_sum(totals)
                for q in range(19):
                    states[number + 1][q, d, OWN, :] = totals[q]
                states[number + 1][19, d, OWN, :] = share_of(d, 0, OWN, inverse, reds)
            else:
                rock = rock_ref[1, d, 0, OWN, :] > 0.5
                label = label_ref[d, 0, OWN, :]
                for q in range(19):
                    first = states[0][q, d, OWN, :]
                    out[0, q, d] = jnp.where(rock, first, totals[q])
                    out[1, q, d] = jnp.where(rock, label * first, reds[q])
    for copy in waiting:
        copy.wait_send()


def body(populations, labels, solid, rates):
    anywhere = pl.BlockSpec(memory_space=pl.ANY)
    field = (2, 2, EXTENT, LANES)
    return pl.pallas_call(
        kernel,
        out_shape=jax.ShapeDtypeStruct((2, 19, 2, ROWS, LANES), jnp.float32),
        in_specs=[pl.BlockSpec(memory_space=pltpu.SMEM)] + [anywhere] * 3,
        out_specs=pl.BlockSpec(memory_space=pltpu.VMEM),
        scratch_shapes=[pltpu.VMEM((FIELDS, 2, EXTENT, LANES), jnp.float32)] * ROUNDS
        + [pltpu.VMEM((2, PACKED, EXTENT, LANES), jnp.float32)] * ROUNDS
        + [
            pltpu.VMEM((ROUNDS, 2, PACKED, ROWS, LANES), jnp.float32),
            pltpu.VMEM((2, 2, ROWS, LANES), jnp.int32),
            pltpu.VMEM((19,) + field, jnp.float32),
            pltpu.VMEM(field, jnp.float32),
            pltpu.VMEM(field, jnp.float32),
            pltpu.VMEM((19,) + field, jnp.float32),
            pltpu.VMEM((19,) + field, jnp.float32),
            pltpu.VMEM(field, jnp.float32),
            pltpu.VMEM((3,) + field, jnp.float32),
            pltpu.SemaphoreType.DMA((ROUNDS, 8)),
            pltpu.SemaphoreType.DMA((ROUNDS, 8)),
            pltpu.SemaphoreType.DMA((3,)),
        ],
        compiler_params=pltpu.CompilerParams(
            collective_id=0, has_side_effects=True, vmem_limit_bytes=32 * 2**20
        ),
    )(rates, populations, labels, solid)


def solution(mesh):
    return jax.shard_map(
        body,
        mesh=mesh,
        in_specs=(P(None, None, "gx", "gy"), P(None, "gx", "gy"), P(None, "gx", "gy"), P()),
        out_specs=P(None, None, None, "gx", "gy"),
        check_vma=False,
    )
```

time: 53.2 us -> 42.4 us (0.80)
  the two profiles are of different devices: /device:TPU:24 before, /device:TPU:1 now
where the time goes in v1:
time: 42.4 us; the launch traced here: 42.1 us
  Pallas kernels  38.4 us (91%)
  local copies, waits for them, and re-layouts  3.68 us (9%)
    pallas_call x1, Pallas kernels, body(): pl.pallas_call(kernel, out_shape=jax.ShapeDtypeStruct((2, 19, 2, ROWS, LA...  38.4 us
    unnamed x9, local copies, waits for them, and re-layouts  3.68 us

profile of v1, /device:TPU:1, one launch (start us, length us, event | category | flops | bytes accessed | tf_op | source)
XLA Modules:
  0.0 42.1 jit_solution(6714702153202624279)
XLA Ops:
  0.0 0.0 copy-start
  0.0 0.9 %copy-done = f32[19,2,8,128]{3,2,1,0:T(8,128)S(1)} copy-done((f32[19,2,8,128]{3,2,1,0:T(8,128)S(1)}, f32[19,2,8,128]{3,2,1,0:T(8,128)}, u32[]{:S(2)}) %copy-start) | copy-done | bytes 155672
  0.9 0.0 copy-start.1
  0.9 0.7 %copy-done.1 = s32[2,8,128]{2,1,0:T(8,128)S(1)} copy-done((s32[2,8,128]{2,1,0:T(8,128)S(1)}, s32[2,8,128]{2,1,0:T(8,128)}, u32[]{:S(2)}) %copy-start.1) | copy-done | bytes 8216
  1.6 0.0 copy-start.2
  1.6 0.7 %copy-done.2 = s32[2,8,128]{2,1,0:T(8,128)S(1)} copy-done((s32[2,8,128]{2,1,0:T(8,128)S(1)}, s32[2,8,128]{2,1,0:T(8,128)}, u32[]{:S(2)}) %copy-start.2) | copy-done | bytes 8216
  2.3 0.0 copy-start.3
  2.3 0.7 %copy-done.3 = f32[15]{0:T(128)S(1)} copy-done((f32[15]{0:T(128)S(1)}, f32[15]{0:T(128)}, u32[]{:S(2)}) %copy-start.3) | copy-done | bytes 84
  3.0 38.4 %shard_map.46 = f32[2,19,2,8,128]{4,3,2,1,0:T(8,128)S(1)} custom-call(f32[15]{0:T(128)S(1)} %copy-done.3, f32[19,2,8,128]{3,2,1,0:T(8,128)S(1)} %copy-done, s32[2,8,128]{2,1,0:T(8,128)S(1)} %copy-done.1, s32[2,8,128]{2,1,0:T(8,128)S(1)} %copy-done.2), custom_call_target="tpu_custom_call" | custom-call | tf_op jit(solution)/shard_map/pallas_call | solution.py:410
  41.4 0.7 %copy.6 = f32[2,19,2,8,128]{4,3,2,1,0:T(8,128)} copy(f32[2,19,2,8,128]{4,3,2,1,0:T(8,128)S(1)} %shard_map.46) | data formatting | bytes 622592
Async XLA Ops:
  0.0 0.9 %copy-start = (f32[19,2,8,128]{3,2,1,0:T(8,128)S(1)}, f32[19,2,8,128]{3,2,1,0:T(8,128)}, u32[]{:S(2)}) copy-start(f32[19,2,8,128]{3,2,1,0:T(8,128)} %pop_hbm.1) | copy-start | bytes 466948
  0.9 0.7 %copy-start.1 = (s32[2,8,128]{2,1,0:T(8,128)S(1)}, s32[2,8,128]{2,1,0:T(8,128)}, u32[]{:S(2)}) copy-start(s32[2,8,128]{2,1,0:T(8,128)} %label_hbm.1) | copy-start | bytes 24580
  1.6 0.7 %copy-start.2 = (s32[2,8,128]{2,1,0:T(8,128)S(1)}, s32[2,8,128]{2,1,0:T(8,128)}, u32[]{:S(2)}) copy-start(s32[2,8,128]{2,1,0:T(8,128)} %solid_hbm.1) | copy-start | bytes 24580
  2.3 0.7 %copy-start.3 = (f32[15]{0:T(128)S(1)}, f32[15]{0:T(128)}, u32[]{:S(2)}) copy-start(f32[15]{0:T(128)} %rate_ref.1) | copy-start | bytes 184

commit v2 on v1

--- a/solution.py
+++ b/solution.py
@@ -43,10 +43,11 @@
 ROWS = 8
 LANES = 128
 EXTENT = ROWS + 2 * HALO
-CHUNK = 8
+CHUNK = 16
 PER_STRIP = LANES // CHUNK
 FIELDS = 21
 PACKED = -(-2 * FIELDS // PER_STRIP)
+PACKED_LATER = -(-2 * (FIELDS - 1) // PER_STRIP)
 OWN = slice(HALO, HALO + ROWS)
 
 
@@ -159,26 +160,18 @@
 
 
 def over_windows(low, high, work):
-    count = -(-(high - low) // ROWS)
-    if count == 1:
-        work(low)
-        return
-
-    def one(index, carry):
-        work(jnp.minimum(low + ROWS * index, high - ROWS))
-        return carry
-
-    lax.fori_loop(0, count, one, 0)
+    for index in range(-(-(high - low) // ROWS)):
+        work(min(low + ROWS * index, high - ROWS))
 
 
 def kernel(
-    rate_ref, pop_hbm, label_hbm, solid_hbm, out, *scratch
+    rate_hbm, pop_hbm, label_hbm, solid_hbm, out, *scratch
 ):
-    states, strips = scratch[:ROUNDS], scratch[ROUNDS : 2 * ROUNDS]
-    packs, codes, left_ref, frac_ref, mix_ref, total_ref, red_ref, label_ref, rock_ref, send, recv, local = scratch[2 * ROUNDS :]
+    states = scratch[:ROUNDS]
+    strips, edges, packs, codes, rate_ref, left_ref, frac_ref, mix_ref, total_ref, red_ref, label_ref, rock_ref, send, recv, local = scratch[ROUNDS:]
     gx, gy = lax.axis_index("gx"), lax.axis_index("gy")
     nx, ny = lax.axis_size("gx"), lax.axis_size("gy")
-    offsets = [(dx, dy) for dy in (1, -1) for dx in (1, -1, 0)] + [(1, 0), (-1, 0)]
+    offsets = [(1, 0), (-1, 0), (0, 1), (0, -1)]
     device = {
         (dx, dy): (lax.rem(gx + (dx + nx), nx), lax.rem(gy + (dy + ny), ny)) for dx, dy in offsets
     }
@@ -186,6 +179,7 @@
     for offset in offsets:
         pl.semaphore_signal(barrier, inc=1, device_id=device[offset], device_id_type=MESH)
     loads = [
+        pltpu.make_async_copy(rate_hbm, rate_ref, local.at[3]),
         pltpu.make_async_copy(label_hbm, codes.at[0], local.at[1]),
         pltpu.make_async_copy(solid_hbm, codes.at[1], local.at[2]),
         pltpu.make_async_copy(pop_hbm, states[0].at[0:19, :, OWN, :], local.at[0]),
@@ -201,54 +195,98 @@
     rate = [rate_ref[k] for k in range(15)]
     lane = lax.broadcasted_iota(jnp.int32, (ROWS, LANES), 1)
     chunk = lane // CHUNK
+    turned_chunk = lax.rem(lane + CHUNK // 2, LANES) // CHUNK
     right_half = lane < LANES // 2
 
-    def pack(number, fields):
-        for first in range(0, 2 * fields, PER_STRIP):
+    def pack():
+        for first in range(0, 2 * FIELDS, PER_STRIP):
             to_left = to_right = None
-            for slot in range(min(PER_STRIP, 2 * fields - first)):
+            for slot in range(min(PER_STRIP, 2 * FIELDS - first)):
                 plane = first + slot
-                value = states[number][plane // 2, plane % 2, OWN, :]
+                value = states[0][plane // 2, plane % 2, OWN, :]
                 moved = value if slot == 0 else pltpu.roll(value, CHUNK * slot, 1)
                 to_left = moved if slot == 0 else jnp.where(chunk == slot, moved, to_left)
                 before = (slot - 1) % PER_STRIP
                 to_right = moved if slot == 0 else jnp.where(chunk == before, moved, to_right)
-            packs[number, 0, first // PER_STRIP] = to_right
-            packs[number, 1, first // PER_STRIP] = to_left
-
-    def exchange(number, fields):
-        copies = []
-        for dx, dy in offsets:
-            begin, low, count = placement(dx)
-            if dy != 0:
-                side, used = (0 if dy > 0 else 1), -(-2 * fields // PER_STRIP)
-                source = packs.at[number, side, 0:used, begin : begin + count, :]
-                target = strips[number].at[side, 0:used, low : low + count, :]
-            else:
-                source = states[number].at[0:fields, :, HALO + begin : HALO + begin + count, :]
-                target = states[number].at[0:fields, :, low : low + count, :]
-            place = len(copies)
-            copy = pltpu.make_async_remote_copy(
-                src_ref=source,
-                dst_ref=target,
-                send_sem=send.at[number, place],
-                recv_sem=recv.at[number, place],
-                device_id=device[dx, dy],
-                device_id_type=MESH,
-            )
-            copy.start()
-            copies.append(copy)
-        for copy in copies:
+            packs[0, first // PER_STRIP] = to_right
+            packs[1, first // PER_STRIP] = to_left
+
+    def pack_edges(planes):
+        for first in range(0, len(planes), PER_STRIP):
+            packed = planes[first]
+            for slot in range(1, min(PER_STRIP, len(planes) - first)):
+                moved = pltpu.roll(planes[first + slot], CHUNK * slot, 1)
+                packed = jnp.where(turned_chunk == slot, moved, packed)
+            edges[0, first // PER_STRIP, OWN, :] = packed
+
+    copies = []
+
+    def push(source, target, offset):
+        place = len(copies)
+        copy = pltpu.make_async_remote_copy(
+            src_ref=source,
+            dst_ref=target,
+            send_sem=send.at[place],
+            recv_sem=recv.at[place],
+            device_id=device[offset],
+            device_id_type=MESH,
+        )
+        copy.start()
+        copies.append(copy)
+        return copy
+
+    def push_rows(number, fields, dx):
+        begin, low, count = placement(dx)
+        share = push(
+            states[number].at[19:fields, :, HALO + begin : HALO + begin + count, :],
+            states[number].at[19:fields, :, low : low + count, :],
+            (dx, 0),
+        )
+        if dx > 0:
+            begin, low = begin + 1, low + 1
+        count = count - 1
+        return [share, push(
+            states[number].at[0:19, :, HALO + begin : HALO + begin + count, :],
+            states[number].at[0:19, :, low : low + count, :],
+            (dx, 0),
+        )]
+
+    def push_strip(dy):
+        side = 0 if dy > 0 else 1
+        return push(packs.at[side], strips.at[side, :, OWN, :], (0, dy))
+
+    def pass_on(strips_ref, dx):
+        begin, low, count = placement(dx)
+        return push(
+            strips_ref.at[:, :, HALO + begin : HALO + begin + count, :],
+            strips_ref.at[:, :, low : low + count, :],
+            (dx, 0),
+        )
+
+    def exchange(number):
+        if number == 0:
+            beside = [push_strip(dy) for dy in (1, -1)]
+        else:
+            rows = [pass_on(edges, dx) for dx in (1, -1)]
+        fields = FIELDS if number == 0 else FIELDS - 1
+        sent = push_rows(number, fields, 1) + push_rows(number, fields, -1)
+        if number == 0:
+            for copy in beside:
+                copy.wait_recv()
+            rows = [pass_on(strips, dx) for dx in (1, -1)]
+        for copy in sent + rows:
             copy.wait_recv()
-        return copies
 
     def strip(number, field, d, rows):
         plane = 2 * field + d
         which, slot = plane // PER_STRIP, plane % PER_STRIP
-        moved = [strips[number][side, which, rows, :] for side in range(2)]
+        if number == 0:
+            moved = [strips[side, which, rows, :] for side in range(2)]
+        else:
+            moved = [edges[0, which, rows, :]]
         if slot:
             moved = [pltpu.roll(value, LANES - CHUNK * slot, 1) for value in moved]
-        return jnp.where(right_half, moved[1], moved[0])
+        return moved[0] if number else jnp.where(right_half, moved[1], moved[0])
 
     def keep(d, part, rows, density, share, remains):
         frac_ref[d, part, rows, :] = share
@@ -372,51 +410,58 @@
                 density, inverse, remains = relax(totals[part], rate)
                 keep(d, part, here, density, share_of(d, part, here, inverse, reds[part]), remains)
 
-    waiting = []
     for number in range(ROUNDS):
-        fields = FIELDS if number == 0 else FIELDS - 1
-        pack(number, fields)
         if number == 0:
+            pack()
             pl.semaphore_wait(barrier, len(offsets))
-        waiting += exchange(number, fields)
+        exchange(number)
         over_windows(0, EXTENT, functools.partial(start, number))
         for step in range(STEPS):
             low, high = 2 * step + 1, EXTENT - 2 * step - 1
             over_windows(low, high, collide)
             if step < STEPS - 1:
                 over_windows(low + 1, high - 1, advance)
-        for d in range(2):
-            totals, reds = stream(HALO, d, 1)
-            totals, reds = totals[0], reds[0]
-            if number < ROUNDS - 1:
-                inverse = 1.0 / weighted_sum(totals)
+        if number < ROUNDS - 1:
+            borders = [None] * (2 * (FIELDS - 1))
+            for d in range(2):
+                totals, reds = stream(HALO, d, 2)
+                share = [
+                    share_of(d, part, OWN, 1.0 / weighted_sum(totals[part]), reds[part]) for part in range(2)
+                ]
                 for q in range(19):
-                    states[number + 1][q, d, OWN, :] = totals[q]
-                states[number + 1][19, d, OWN, :] = share_of(d, 0, OWN, inverse, reds)
-            else:
+                    states[number + 1][q, d, OWN, :] = totals[0][q]
+                    borders[2 * q + d] = totals[1][q]
+                states[number + 1][19, d, OWN, :] = share[0]
+                borders[2 * 19 + d] = share[1]
+            pack_edges(borders)
+        else:
+            for d in range(2):
+                totals, reds = stream(HALO, d, 1)
                 rock = rock_ref[1, d, 0, OWN, :] > 0.5
                 label = label_ref[d, 0, OWN, :]
                 for q in range(19):
                     first = states[0][q, d, OWN, :]
-                    out[0, q, d] = jnp.where(rock, first, totals[q])
-                    out[1, q, d] = jnp.where(rock, label * first, reds[q])
-    for copy in waiting:
+                    out[0, q, d] = jnp.where(rock, first, totals[0][q])
+                    out[1, q, d] = jnp.where(rock, label * first, reds[0][q])
+    for copy in copies:
         copy.wait_send()
 
 
 def body(populations, labels, solid, rates):
-    anywhere = pl.BlockSpec(memory_space=pl.ANY)
+    in_place = pl.BlockSpec(memory_space=pl.ANY)
     field = (2, 2, EXTENT, LANES)
     return pl.pallas_call(
         kernel,
         out_shape=jax.ShapeDtypeStruct((2, 19, 2, ROWS, LANES), jnp.float32),
-        in_specs=[pl.BlockSpec(memory_space=pltpu.SMEM)] + [anywhere] * 3,
+        in_specs=[in_place] * 4,
         out_specs=pl.BlockSpec(memory_space=pltpu.VMEM),
         scratch_shapes=[pltpu.VMEM((FIELDS, 2, EXTENT, LANES), jnp.float32)] * ROUNDS
-        + [pltpu.VMEM((2, PACKED, EXTENT, LANES), jnp.float32)] * ROUNDS
         + [
-            pltpu.VMEM((ROUNDS, 2, PACKED, ROWS, LANES), jnp.float32),
+            pltpu.VMEM((2, PACKED, EXTENT, LANES), jnp.float32),
+            pltpu.VMEM((1, PACKED_LATER, EXTENT, LANES), jnp.float32),
+            pltpu.VMEM((2, PACKED, ROWS, LANES), jnp.float32),
             pltpu.VMEM((2, 2, ROWS, LANES), jnp.int32),
+            pltpu.SMEM((15,), jnp.float32),
             pltpu.VMEM((19,) + field, jnp.float32),
             pltpu.VMEM(field, jnp.float32),
             pltpu.VMEM(field, jnp.float32),
@@ -424,14 +469,14 @@
             pltpu.VMEM((19,) + field, jnp.float32),
             pltpu.VMEM(field, jnp.float32),
             pltpu.VMEM((3,) + field, jnp.float32),
-            pltpu.SemaphoreType.DMA((ROUNDS, 8)),
-            pltpu.SemaphoreType.DMA((ROUNDS, 8)),
-            pltpu.SemaphoreType.DMA((3,)),
+            pltpu.SemaphoreType.DMA((20,)),
+            pltpu.SemaphoreType.DMA((20,)),
+            pltpu.SemaphoreType.DMA((4,)),
         ],
         compiler_params=pltpu.CompilerParams(
             collective_id=0, has_side_effects=True, vmem_limit_bytes=32 * 2**20
         ),
-    )(rates, populations, labels, solid)
+    )(*[pltpu.with_memory_space_constraint(x, pltpu.HBM) for x in (rates, populations, labels, solid)])
 
 
 def solution(mesh):

time: 42.4 us -> 35.1 us (0.83)
  the two profiles are of different devices: /device:TPU:1 before, /device:TPU:24 now
where the time goes in v2:
time: 35.1 us; the launch traced here: 34.9 us
  Pallas kernels  34.2 us (97%)
  local copies, waits for them, and re-layouts  0.72 us (2%)
    pallas_call x1, Pallas kernels, body(): pl.pallas_call(kernel, out_shape=jax.ShapeDtypeStruct((2, 19, 2, ROWS, LA...  34.2 us
    unnamed x1, local copies, waits for them, and re-layouts  0.72 us

profile of v2, /device:TPU:24, one launch (start us, length us, event | category | flops | bytes accessed | tf_op | source)
XLA Modules:
  0.0 34.9 jit_solution(14002614724411621976)
XLA Ops:
  0.0 34.2 %shard_map.46 = f32[2,19,2,8,128]{4,3,2,1,0:T(8,128)S(1)} custom-call(f32[15]{0:T(128)} %rate_hbm.1, f32[19,2,8,128]{3,2,1,0:T(8,128)} %pop_hbm.1, s32[2,8,128]{2,1,0:T(8,128)} %label_hbm.1, s32[2,8,128]{2,1,0:T(8,128)} %solid_hbm.1), custom_call_target="tpu_custom_call" | custom-call | tf_op jit(solution)/shard_map/pallas_call | solution.py:453
  34.2 0.7 %copy.6 = f32[2,19,2,8,128]{4,3,2,1,0:T(8,128)} copy(f32[2,19,2,8,128]{4,3,2,1,0:T(8,128)S(1)} %shard_map.46) | data formatting | bytes 622592

commit v3 on v2

--- a/solution.py
+++ b/solution.py
@@ -43,7 +43,7 @@
 ROWS = 8
 LANES = 128
 EXTENT = ROWS + 2 * HALO
-CHUNK = 16
+CHUNK = 12
 PER_STRIP = LANES // CHUNK
 FIELDS = 21
 PACKED = -(-2 * FIELDS // PER_STRIP)
@@ -255,27 +255,13 @@
         side = 0 if dy > 0 else 1
         return push(packs.at[side], strips.at[side, :, OWN, :], (0, dy))
 
-    def pass_on(strips_ref, dx):
+    def pass_on(strips_ref, dx, side):
         begin, low, count = placement(dx)
         return push(
-            strips_ref.at[:, :, HALO + begin : HALO + begin + count, :],
-            strips_ref.at[:, :, low : low + count, :],
+            strips_ref.at[side, :, HALO + begin : HALO + begin + count, :],
+            strips_ref.at[side, :, low : low + count, :],
             (dx, 0),
         )
-
-    def exchange(number):
-        if number == 0:
-            beside = [push_strip(dy) for dy in (1, -1)]
-        else:
-            rows = [pass_on(edges, dx) for dx in (1, -1)]
-        fields = FIELDS if number == 0 else FIELDS - 1
-        sent = push_rows(number, fields, 1) + push_rows(number, fields, -1)
-        if number == 0:
-            for copy in beside:
-                copy.wait_recv()
-            rows = [pass_on(strips, dx) for dx in (1, -1)]
-        for copy in sent + rows:
-            copy.wait_recv()
 
     def strip(number, field, d, rows):
         plane = 2 * field + d
@@ -294,26 +280,54 @@
         for q in range(19):
             left_ref[q, d, part, rows, :] = remains[q]
 
-    def start(number, row):
+    def start(number, part, row):
         rows = pl.ds(row, ROWS)
         for d in range(2):
 
-            def both_of(field):
-                return [states[number][field, d, rows, :], strip(number, field, d, rows)]
-
-            share = both_of(19)
+            def cells(field):
+                return states[number][field, d, rows, :] if part == 0 else strip(number, field, d, rows)
+
+            share = cells(19)
             if number == 0:
-                rock = both_of(20)
-                for dy in (-1, 0, 1):
-                    moved = lateral(rock, dy, lane)
-                    for part in range(2):
-                        rock_ref[dy + 1, d, part, rows, :] = moved[part]
+                label_ref[d, part, rows, :] = share
+            density, _, remains = relax([cells(q) for q in range(19)], rate)
+            keep(d, part, rows, density, share, remains)
+
+    def walls(row):
+        rows = pl.ds(row, ROWS)
+        for d in range(2):
+            rock = [states[0][20, d, rows, :], strip(0, 20, d, rows)]
+            for dy in (-1, 0, 1):
+                moved = lateral(rock, dy, lane)
                 for part in range(2):
-                    label_ref[d, part, rows, :] = share[part]
-            f = [both_of(q) for q in range(19)]
-            for part in range(2):
-                density, _, remains = relax([pair[part] for pair in f], rate)
-                keep(d, part, rows, density, share[part], remains)
+                    rock_ref[dy + 1, d, part, rows, :] = moved[part]
+
+    def begin_round(number):
+        outer = (0, EXTENT - ROWS)
+        if number == 0:
+            beside = [push_strip(dy) for dy in (1, -1)]
+            sent = push_rows(0, FIELDS, 1) + push_rows(0, FIELDS, -1)
+            start(0, 0, HALO)
+            corners = []
+            for side, copy in enumerate(beside):
+                copy.wait_recv()
+                corners += [pass_on(strips, dx, side) for dx in (1, -1)]
+            start(0, 1, HALO)
+        else:
+            corners = [pass_on(edges, dx, 0) for dx in (1, -1)]
+            sent = push_rows(number, FIELDS - 1, 1) + push_rows(number, FIELDS - 1, -1)
+            start(number, 0, HALO)
+            start(number, 1, HALO)
+        for copy in sent:
+            copy.wait_recv()
+        for row in outer:
+            start(number, 0, row)
+        for copy in corners:
+            copy.wait_recv()
+        for row in outer:
+            start(number, 1, row)
+        if number == 0:
+            over_windows(0, EXTENT, walls)
 
     def collide(row):
         here = pl.ds(row, ROWS)
@@ -414,8 +428,7 @@
         if number == 0:
             pack()
             pl.semaphore_wait(barrier, len(offsets))
-        exchange(number)
-        over_windows(0, EXTENT, functools.partial(start, number))
+        begin_round(number)
         for step in range(STEPS):
             low, high = 2 * step + 1, EXTENT - 2 * step - 1
             over_windows(low, high, collide)

time: 35.1 us -> 34 us (0.969)
  Pallas kernels: 34.2 us -> 33.1 us
    pallas_call x1, Pallas kernels: 34.2 us -> 33.1 us  [body(): pl.pallas_call(kernel, out_shape=jax.ShapeDtypeStruct((2, 19, 2, ROWS, LA...]
where the time goes in v3:
time: 34 us; the launch traced here: 33.9 us
  Pallas kernels  33.1 us (97%)
  local copies, waits for them, and re-layouts  0.72 us (2%)
    pallas_call x1, Pallas kernels, body(): pl.pallas_call(kernel, out_shape=jax.ShapeDtypeStruct((2, 19, 2, ROWS, LA...  33.1 us
    unnamed x1, local copies, waits for them, and re-layouts  0.72 us

profile of v3, /device:TPU:24, one launch (start us, length us, event | category | flops | bytes accessed | tf_op | source)
XLA Modules:
  0.0 33.9 jit_solution(10008638592034908005)
XLA Ops:
  0.0 33.1 %shard_map.46 = f32[2,19,2,8,128]{4,3,2,1,0:T(8,128)S(1)} custom-call(f32[15]{0:T(128)} %rate_hbm.1, f32[19,2,8,128]{3,2,1,0:T(8,128)} %pop_hbm.1, s32[2,8,128]{2,1,0:T(8,128)} %label_hbm.1, s32[2,8,128]{2,1,0:T(8,128)} %solid_hbm.1), custom_call_target="tpu_custom_call" | custom-call | tf_op jit(solution)/shard_map/pallas_call | solution.py:466
  33.2 0.7 %copy.6 = f32[2,19,2,8,128]{4,3,2,1,0:T(8,128)} copy(f32[2,19,2,8,128]{4,3,2,1,0:T(8,128)S(1)} %shard_map.46) | data formatting | bytes 622592
